TPU v7x, 512 devices: a whole 4x8x8 slice. The times are simulated.
512 devices in a mesh: section: 16 (over x_hi, z), peer: 32 (over y, x_lo, core).
Axes of the slice: x: 4 (x_hi: 2, x_lo: 2; x = x_hi * 2 + x_lo), y: 8, z: 8, core: 2. Of those that a mesh axis runs over, the one named last changes fastest.
Arguments:
- acts: bfloat16 [16, 32, 2, 64, 2560], P('section', 'peer'), may hold values from -6 to 6
- cotangent: bfloat16 [16, 32, 2, 64, 2560], P('section', 'peer'), may hold values from -6 to 6
- gain: float32 [16, 2560], P('section'), may hold values from 0.1 to 1.9
- w_down: bfloat16 [16, 2560, 128], P('section'), may hold values from -0.125 to 0.125
- w_up: bfloat16 [16, 128, 2560], P('section'), may hold values from -0.5 to 0.5
- route_fwd: int32 [16, 32, 2], P('section', 'peer'), may hold values from 0 to 31, as said below
- route_bwd: int32 [16, 32, 2], P('section', 'peer'), may hold values from 0 to 31, as said below
- token_counts: int32 [16, 32, 2], P('section', 'peer'), may hold values from 1 to 64, as said below
Outputs:
- arrived_act: bfloat16 [16, 32, 3, 64, 2560], P('section', 'peer')
- arrived_grad: bfloat16 [16, 32, 3, 64, 2560], P('section', 'peer')
- grad_down: float32 [16, 2560, 128], P('section', 'peer')
- grad_up: float32 [16, 128, 2560], P('section', None, 'peer')
- grad_gain: float32 [16, 2560], P('section', 'peer')
Inputs may be any that keep to these rules, and one draw needn't show every extreme that they name: route_fwd[s, p, j] is a peer of section s + 1; the 2 entries of one peer differ; at every section boundary no peer is named more than 3 times and some peer exactly 3 times. route_bwd[s, p, j] is a peer of section s - 1, with the same rules as route_fwd. `token_counts`: some micro-batch holds exactly 64 live tokens.
All inputs are finite; a program needn't handle non-finite values.
Results may differ from a plain program's by a relative error of at most 0.0053.
Values may be sent and summed in bfloat16 or wider, within the bound.
A program may use at most 128 MiB of HBM per device.

v0:
```python
import jax
import jax.numpy as jnp
from jax import lax
from jax.sharding import PartitionSpec as P

epsilon = 1e-05


def from_behind(block, axis, distance):
    devices = range(lax.axis_size(axis))
    route = [(i - distance, i) for i in devices if i - distance in devices]
    return lax.ppermute(block, axis, route)


def adapter_forward(rows, token_mask, gain_row, down_proj, up_proj):
    widened = rows.astype(jnp.float32)
    inverse = lax.rsqrt(jnp.mean(widened * widened, axis=-1, keepdims=True) + epsilon)
    unit_rows = widened * inverse
    normed = (unit_rows * gain_row[None, :]).astype(jnp.bfloat16)
    before = jnp.dot(normed, down_proj, preferred_element_type=jnp.float32)
    active = jax.nn.silu(before).astype(jnp.bfloat16)
    branch = jnp.dot(active, up_proj, preferred_element_type=jnp.float32)
    outputs = ((widened + branch) * token_mask[:, None]).astype(jnp.bfloat16)
    return (outputs, (inverse, unit_rows, normed, before, active))


def adapter_backward(incoming, token_mask, gain_row, down_proj, up_proj, saved_state):
    inverse, unit_rows, normed, before, active = saved_state
    masked = incoming * token_mask[:, None].astype(jnp.bfloat16)
    up_total = jnp.dot(active.T, masked, preferred_element_type=jnp.float32)
    act_grad = jnp.dot(masked, up_proj.T, preferred_element_type=jnp.float32)
    sig_value = jax.nn.sigmoid(before)
    pre_grad = (act_grad * sig_value * (1.0 + before * (1.0 - sig_value))).astype(jnp.bfloat16)
    down_total = jnp.dot(normed.T, pre_grad, preferred_element_type=jnp.float32)
    norm_grad = jnp.dot(pre_grad, down_proj.T, preferred_element_type=jnp.float32)
    gain_total = jnp.sum(norm_grad * unit_rows, axis=0)
    unit_grad = norm_grad * gain_row[None, :]
    input_grad = masked.astype(jnp.float32) + inverse * (
        unit_grad - unit_rows * jnp.mean(unit_grad * unit_rows, axis=-1, keepdims=True)
    )
    return (input_grad.astype(jnp.bfloat16), down_total, up_total, gain_total)


def spread_rows(values, token_flags, targets, peer_count):
    choose = (
        targets.astype(jnp.float32)[:, None] == jnp.arange(peer_count, dtype=jnp.float32)[None, :]
    ).astype(jnp.bfloat16)
    buffer = jnp.einsum("jp,jtd->ptd", choose, values, preferred_element_type=jnp.float32).astype(
        jnp.bfloat16
    )
    flag_buffer = jnp.einsum(
        "jp,jt->pt", choose, token_flags, preferred_element_type=jnp.float32
    ).astype(jnp.bfloat16)
    return (buffer, flag_buffer)


def compact_rows(received, received_flags, capacity):
    present = (received_flags[:, 0] > 0).astype(jnp.float32)
    position = jnp.cumsum(present) - 1.0
    slot_ids = jnp.arange(capacity, dtype=jnp.float32)
    pick_table = (
        (position[None, :] == slot_ids[:, None]).astype(jnp.float32) * present[None, :]
    ).astype(jnp.bfloat16)
    return jnp.einsum(
        "kq,qtd->ktd", pick_table, received, preferred_element_type=jnp.float32
    ).astype(jnp.bfloat16)


def on_device(acts, cotangent, gain, w_down, w_up, route_fwd, route_bwd, token_counts):
    peer_count = lax.axis_size("peer")
    blocks = acts.shape[2]
    length = acts.shape[3]
    model_width = acts.shape[4]
    capacity = blocks + blocks // 2
    positions = lax.broadcasted_iota(jnp.int32, (blocks, length), 1)
    mask_grid = (positions < token_counts[0, 0][:, None]).astype(jnp.float32)
    token_mask = mask_grid.reshape(-1)
    outputs, saved_state = adapter_forward(
        acts[0, 0].reshape(-1, model_width), token_mask, gain[0], w_down[0], w_up[0]
    )
    input_grad, down_total, up_total, gain_total = adapter_backward(
        cotangent[0, 0].reshape(-1, model_width),
        token_mask,
        gain[0],
        w_down[0],
        w_up[0],
        saved_state,
    )
    outputs = outputs.reshape(blocks, length, model_width)
    input_grad = input_grad.reshape(blocks, length, model_width)
    token_flags = mask_grid.astype(jnp.bfloat16)
    ahead_targets = route_fwd[0, 0].astype(jnp.bfloat16)
    behind_targets = route_bwd[0, 0].astype(jnp.bfloat16)
    grad_down, grad_up, grad_gain = (
        lax.psum_scatter(down_total, "peer", scatter_dimension=0, tiled=True),
        lax.psum_scatter(up_total, "peer", scatter_dimension=1, tiled=True),
        lax.psum_scatter(gain_total, "peer", scatter_dimension=0, tiled=True),
    )
    buffer, flag_buffer = spread_rows(outputs, token_flags, ahead_targets, peer_count)
    received, received_flags = (
        lax.all_to_all(buffer, "peer", split_axis=0, concat_axis=0, tiled=True),
        lax.all_to_all(flag_buffer, "peer", split_axis=0, concat_axis=0, tiled=True),
    )
    arrived_act = from_behind(compact_rows(received, received_flags, capacity), "section", 1)
    buffer, flag_buffer = spread_rows(input_grad, token_flags, behind_targets, peer_count)
    received, received_flags = (
        lax.all_to_all(buffer, "peer", split_axis=0, concat_axis=0, tiled=True),
        lax.all_to_all(flag_buffer, "peer", split_axis=0, concat_axis=0, tiled=True),
    )
    arrived_grad = from_behind(compact_rows(received, received_flags, capacity), "section", -1)
    return (
        arrived_act[None, None],
        arrived_grad[None, None],
        (grad_down / peer_count)[None],
        (grad_up / peer_count)[None],
        (grad_gain / peer_count)[None],
    )


def solution(mesh):
    placed = (
        P("section", "peer", None, None, None),
        P("section", "peer", None, None, None),
        P("section", None),
        P("section", None, None),
        P("section", None, None),
        P("section", "peer", None),
        P("section", "peer", None),
        P("section", "peer", None),
    )
    return jax.shard_map(
        on_device,
        mesh=mesh,
        in_specs=placed,
        out_specs=(
            P("section", "peer", None, None, None),
            P("section", "peer", None, None, None),
            P("section", "peer", None),
            P("section", None, "peer"),
            P("section", "peer"),
        ),
        check_vma=False,
    )
```

profile of v0, /device:TPU:27, one launch (start us, length us, event | category | flops | bytes accessed | tf_op | source)
XLA Modules:
  0.0 691.6 jit_solution(1120397349616957638)
XLA Ops:
  7.2 0.8 bitcast_convert_fusion.1
  8.0 0.9 fusion.14
  8.9 0.6 copy.27
  9.5 9.5 %all-to-all-start = ((bf16[32,1,64]{2,1,0:T(2,128)(2,1)}), bf16[32,1,64]{2,1,0:T(2,128)(2,1)S(1)}, u32[]{:S(2)}, u32[]{:S(2)}) async-start(bf16[32,1,64]{2,1,0:T(2,128)(2,1)} %copy.27), calls=%async_computation | async-start | bytes 32768 | tf_op jit(solution)/shard_map/all_to_all | solution.py:102
  18.9 0.7 fusion.45
  19.7 0.7 bitcast_convert_fusion
  20.3 1.3 multiply_reduce_fusion.2
  21.8 0.7 reduce.3
  22.6 0.2 multiply_convert_fusion.1
  22.8 0.3 fusion.20
  23.2 0.5 copy-done.3
  23.7 0.1 broadcast_multiply_fusion
  23.8 0.2 copy-done.4
  24.0 0.3 fusion.13
  24.3 0.6 multiply_reduce_fusion
  24.9 0.6 add_convert_fusion
  25.5 0.1 copy-done.5
  25.6 0.3 fusion.15
  25.8 0.6 copy.32
  26.4 8.3 %all-to-all-start.2 = ((bf16[32,1,64]{2,1,0:T(2,128)(2,1)}), bf16[32,1,64]{2,1,0:T(2,128)(2,1)S(1)}, u32[]{:S(2)}, u32[]{:S(2)}) async-start(bf16[32,1,64]{2,1,0:T(2,128)(2,1)} %copy.32), calls=%async_computation.2 | async-start | bytes 32768 | tf_op jit(solution)/shard_map/all_to_all | solution.py:108
  34.8 5.7 convolution_convert_fusion
  40.5 13.7 %copy.34 = bf16[32,64,2560]{2,1,0:T(8,128)(2,1)} copy(bf16[32,64,2560]{2,0,1:T(8,128)(2,1)} %convolution_convert_fusion) | data formatting | bytes 20971520 | tf_op jit(solution)/shard_map/convert_element_type | solution.py:48
  54.2 9.0 %all-to-all-start.3 = ((bf16[32,64,2560]{2,1,0:T(8,128)(2,1)}), bf16[32,64,2560]{2,1,0:T(8,128)(2,1)}, u32[]{:S(2)}, u32[]{:S(2)}) async-start(bf16[32,64,2560]{2,1,0:T(8,128)(2,1)} %copy.34), calls=%async_computation.3 | async-start | bytes 20971520 | tf_op jit(solution)/shard_map/all_to_all | solution.py:107
  63.2 0.3 fusion.11
  63.5 5.8 convolution_convert_fusion.1
  69.3 13.6 %copy.29 = bf16[32,64,2560]{2,1,0:T(8,128)(2,1)} copy(bf16[32,64,2560]{2,0,1:T(8,128)(2,1)} %convolution_convert_fusion.1) | data formatting | bytes 20971520 | tf_op jit(solution)/shard_map/convert_element_type | solution.py:48
  82.9 207.9 %all-to-all-done.3 = bf16[32,64,2560]{2,1,0:T(8,128)(2,1)} async-done(((bf16[32,64,2560]{2,1,0:T(8,128)(2,1)}), bf16[32,64,2560]{2,1,0:T(8,128)(2,1)}, u32[]{:S(2)}, u32[]{:S(2)}) %all-to-all-start.3) | async-done | bytes 10485792 | tf_op jit(solution)/shard_map/all_to_all | solution.py:107
  290.8 8.9 %all-to-all-start.1 = ((bf16[32,64,2560]{2,1,0:T(8,128)(2,1)}), bf16[32,64,2560]{2,1,0:T(8,128)(2,1)}, u32[]{:S(2)}, u32[]{:S(2)}) async-start(bf16[32,64,2560]{2,1,0:T(8,128)(2,1)} %copy.29), calls=%async_computation.1 | async-start | bytes 20971520 | tf_op jit(solution)/shard_map/all_to_all | solution.py:101
  299.7 1.5 fusion.48
  301.2 0.2 reduce-scatter.3.cloned.1.call-start
  301.4 1.4 fusion.49
  303.1 0.1 add_reduce_fusion
  303.2 0.1 add_reduce_fusion.1
  303.3 15.6 %fusion.7 = bf16[3,64,2560]{2,0,1:T(4,128)(2,1)S(1)} fusion(bf16[32,64,2560]{2,1,0:T(8,128)(2,1)} %all-to-all-done.3, bf16[32]{0:T(256)(128)(2,1)S(1)} %get-tuple-element.26, f32[32]{0:T(128)S(1)} %get-tuple-element.25), kind=kOutput, calls=%fused_computation.7 | convolution fusion | flops 31948992 | bytes 11468992 | tf_op jit(solution)/shard_map/kq,qtd->ktd/dot_general | solution.py:64
  318.9 0.2 copy.36
  319.1 1.3 collective-permute-start.1
  320.4 206.4 %all-to-all-done.1 = bf16[32,64,2560]{2,1,0:T(8,128)(2,1)} async-done(((bf16[32,64,2560]{2,1,0:T(8,128)(2,1)}), bf16[32,64,2560]{2,1,0:T(8,128)(2,1)}, u32[]{:S(2)}, u32[]{:S(2)}) %all-to-all-start.1) | async-done | bytes 10485792 | tf_op jit(solution)/shard_map/all_to_all | solution.py:101
  526.8 15.3 %fusion.4 = bf16[3,64,2560]{2,0,1:T(4,128)(2,1)S(1)} fusion(bf16[32,64,2560]{2,1,0:T(8,128)(2,1)} %all-to-all-done.1, bf16[32]{0:T(256)(128)(2,1)S(1)} %get-tuple-element.24, f32[32]{0:T(128)S(1)} %get-tuple-element.23), kind=kOutput, calls=%fused_computation.6 | convolution fusion | flops 31948992 | bytes 11468992 | tf_op jit(solution)/shard_map/kq,qtd->ktd/dot_general | solution.py:64
  542.1 1.2 copy.31
  543.3 4.4 collective-permute-start
  547.7 1.3 dynamic-slice
  549.6 123.8 %all-reduce = f32[2560]{0:T(1024)S(1)} all-reduce(f32[2560]{0:T(1024)S(1)} %get-tuple-element.15), channel_id=4, replica_groups=mesh['section'=16,'peer'=32] {'peer'}, use_global_device_ids=true, to_apply=%region_7.8.clone | all-reduce | flops 2560 | bytes 20480
  673.3 0.6 fusion.38
  673.9 1.4 multiply_bitcast_fusion
  675.3 4.4 reduce-scatter.3.cloned.1.call-done
  679.7 1.4 multiply_bitcast_fusion.1
  681.1 2.3 copy.57
  683.4 0.9 copy.58
  (28 shorter events, 0.4 us)
Async XLA Ops:
  7.2 15.6 %copy-start = (bf16[1,2560,128]{2,1,0:T(8,128)(2,1)S(1)}, bf16[1,2560,128]{2,1,0:T(8,128)(2,1)}, u32[]{:S(2)}) copy-start(bf16[1,2560,128]{2,1,0:T(8,128)(2,1)} %param.11) | copy-start | bytes 1966084
  7.2 15.4 %copy-start.2 = (bf16[1,1,2,64,2560]{4,3,2,1,0:T(8,128)(2,1)S(1)}, bf16[1,1,2,64,2560]{4,3,2,1,0:T(8,128)(2,1)}, u32[]{:S(2)}) copy-start(bf16[1,1,2,64,2560]{4,3,2,1,0:T(8,128)(2,1)} %param.8) | copy-start | bytes 1966084
  9.5 17.0 %all-to-all-start = ((bf16[32,1,64]{2,1,0:T(2,128)(2,1)}), bf16[32,1,64]{2,1,0:T(2,128)(2,1)S(1)}, u32[]{:S(2)}, u32[]{:S(2)}) async-start(bf16[32,1,64]{2,1,0:T(2,128)(2,1)} %copy.27), calls=%async_computation | async-start | bytes 32768 | tf_op jit(solution)/shard_map/all_to_all | solution.py:102
  22.6 1.1 copy-start.3
  22.8 1.1 copy-start.4
  24.9 0.7 copy-start.5
  26.4 27.8 %all-to-all-start.2 = ((bf16[32,1,64]{2,1,0:T(2,128)(2,1)}), bf16[32,1,64]{2,1,0:T(2,128)(2,1)S(1)}, u32[]{:S(2)}, u32[]{:S(2)}) async-start(bf16[32,1,64]{2,1,0:T(2,128)(2,1)} %copy.32), calls=%async_computation.2 | async-start | bytes 32768 | tf_op jit(solution)/shard_map/all_to_all | solution.py:108
  54.2 236.6 %all-to-all-start.3 = ((bf16[32,64,2560]{2,1,0:T(8,128)(2,1)}), bf16[32,64,2560]{2,1,0:T(8,128)(2,1)}, u32[]{:S(2)}, u32[]{:S(2)}) async-start(bf16[32,64,2560]{2,1,0:T(8,128)(2,1)} %copy.34), calls=%async_computation.3 | async-start | bytes 20971520 | tf_op jit(solution)/shard_map/all_to_all | solution.py:107
  290.8 236.0 %all-to-all-start.1 = ((bf16[32,64,2560]{2,1,0:T(8,128)(2,1)}), bf16[32,64,2560]{2,1,0:T(8,128)(2,1)}, u32[]{:S(2)}, u32[]{:S(2)}) async-start(bf16[32,64,2560]{2,1,0:T(8,128)(2,1)} %copy.29), calls=%async_computation.1 | async-start | bytes 20971520 | tf_op jit(solution)/shard_map/all_to_all | solution.py:101
  299.7 374.2 %reduce-scatter.5.cloned.1.call-start = ((), (), s32[]{:S(2)}) async-start(), calls=%async_computation.7 | async-start | bytes 1351680 | tf_op jit(solution)/shard_map/reduce_scatter | solution.py:96
  301.2 378.5 %reduce-scatter.3.cloned.1.call-start = ((), (), s32[]{:S(2)}) async-start(), calls=%async_computation.6 | async-start | bytes 1351680 | tf_op jit(solution)/shard_map/reduce_scatter | solution.py:95
  319.1 362.1 %collective-permute-start.1 = (bf16[3,64,2560]{2,1,0:T(8,128)(2,1)S(1)}, bf16[3,64,2560]{2,1,0:T(8,128)(2,1)S(1)}, u32[]{:S(2)}, u32[]{:S(2)}) collective-permute-start(bf16[3,64,2560]{2,1,0:T(8,128)(2,1)S(1)} %copy.36), channel_id=1, source_target_pairs={{32,0},{64,32},{96,64},{128,96},{160,128},{192,160},{224,192},{256... | collective-permute-start | bytes 2949128 | tf_op jit(solution)/shard_map/ppermute | solution.py:12
  543.3 137.8 %collective-permute-start = (bf16[3,64,2560]{2,1,0:T(8,128)(2,1)}, bf16[3,64,2560]{2,1,0:T(8,128)(2,1)}, u32[]{:S(2)}, u32[]{:S(2)}) collective-permute-start(bf16[3,64,2560]{2,1,0:T(8,128)(2,1)} %copy.31), channel_id=1, source_target_pairs={{0,32},{32,64},{64,96},{96,128},{128,160},{160,192},{192,224},{224... | collective-permute-start | bytes 2949128 | tf_op jit(solution)/shard_map/ppermute | solution.py:12
  681.1 3.2 copy-start.1
Sparse Core Ops, SparseCore 0:
  303.3 180.4 reduce-scatter.4
  486.9 192.8 reduce-scatter.2
where the time goes:
time: 701 us; the launch traced here: 692 us
  waiting for transfers between devices  419 us (60%)
  blocking collectives  124 us (18%)
  matrix products  48.1 us (7%)
  starting transfers between devices  41.5 us (6%)
  local copies, waits for them, and re-layouts  35.4 us (5%)
  between operations  15.2 us (2%)
  other arithmetic  8.84 us (1%)
    all_to_all x2, waiting for transfers between devices, on_device(): lax.all_to_all(buffer, 'peer', split_axis=0, concat_axis=0, tiled=True)  414 us
    unnamed x1, blocking collectives  124 us
    dot_general x2, matrix products, compact_rows(): jnp.einsum('kq,qtd->ktd', pick_table, received, preferred_element_type=jn...  30.9 us
    convert_element_type x2, local copies, waits for them, and re-layouts, spread_rows(): jnp.einsum('jp,jtd->ptd', choose, values, preferred_element_type=jnp.floa...  27.3 us
    all_to_all x2, starting transfers between devices, on_device(): lax.all_to_all(buffer, 'peer', split_axis=0, concat_axis=0, tiled=True)  17.9 us
    all_to_all x2, starting transfers between devices, on_device(): lax.all_to_all(flag_buffer, 'peer', split_axis=0, concat_axis=0, tiled=True)  17.8 us
  transfers between devices with their start and end apart: 8, of which 3 were waited for; matrix products, arithmetic and copies ran while one was open for 12% of the time, Pallas kernels for 0%

commit v1 on v0

v1 whole, which is shorter than its diff:
```python
import functools

import jax
import jax.numpy as jnp
from jax import lax
from jax.experimental import pallas as pl
from jax.experimental.pallas import tpu as pltpu
from jax.sharding import PartitionSpec as P

epsilon = 1e-05
MESH = pl.DeviceIdType.MESH
f32, bf16, i32 = jnp.float32, jnp.bfloat16, jnp.int32


def matmul(a, b, contract_a, contract_b):
    return lax.dot_general(
        a, b, (((contract_a,), (contract_b,)), ((), ())), preferred_element_type=f32
    )


def arrived(ref, sem):
    pltpu.make_async_copy(ref, ref, sem).wait()


def kernel(
    sections, peers, cap,
    route_fwd, route_bwd, counts, x_ref, cot_ref, gain_ref, down_ref, up_ref,
    act_out, grad_out, gdown_out, gup_out, ggain_out,
    normed, masked, norm_grad, inverse, gain_acc,
    src_f, src_b, mid_f, mid_b, pick_f, pick_b,
    tile_f, tile_b, tiles_f, tiles_b, table_v, table_f, table_b,
    piece, from_core, from_x, chain_a, chain_b,
    p1_send, p1_recv, swap_send, swap_recv, tile_send, tile_recv,
    tswap_send, tswap_recv, table_sem, p2_send, p2_recv,
    core_send, core_recv, x_send, x_recv, a_send, a_recv, b_send, b_recv,
):
    rows, width = x_ref.shape
    units = up_ref.shape[0]
    spread, batches, group, span = src_f.shape
    ring = spread // 2
    column_groups = width // span
    row_groups = spread // column_groups
    share = width // peers
    length = rows // batches

    s, p = lax.axis_index("section"), lax.axis_index("peer")
    c, m = p % 2, p // 2
    x, y = m % 2, m // 2
    sibling = p + 1 - 2 * c
    has_next = s < sections - 1
    has_prev = s > 0

    def partner(i):
        k = i // 2
        odd = k % 2
        step = odd * ((k + 1) // 2) + (1 - odd) * (ring - k // 2)
        return ((y + step) % ring) * 2 + (x + i) % 2

    barrier = pltpu.get_barrier_semaphore()

    def greet(i, carry):
        q = 2 * partner(i) + c

        @pl.when(has_next)
        def _():
            pl.semaphore_signal(barrier, inc=1, device_id=(s + 1, q), device_id_type=MESH)

        @pl.when(has_prev)
        def _():
            pl.semaphore_signal(barrier, inc=1, device_id=(s - 1, q), device_id_type=MESH)

        @pl.when(i > 0)
        def _():
            pl.semaphore_signal(barrier, inc=1, device_id=(s, q), device_id_type=MESH)

        return carry

    lax.fori_loop(0, spread, greet, 0)
    pl.semaphore_signal(barrier, inc=1, device_id=(s, sibling), device_id_type=MESH)

    row_ids = lax.broadcasted_iota(i32, (rows, 1), 0)
    limit = jnp.where(row_ids < length, counts[0], counts[1] + length)
    mask = (row_ids < limit).astype(f32)
    mask_small = mask.astype(bf16)

    def normalise(g, carry):
        here = pl.ds(pl.multiple_of(g * group, group), group)
        widened = x_ref[here, :].astype(f32)
        inv = lax.rsqrt(jnp.sum(widened * widened, axis=-1, keepdims=True) / width + epsilon)
        inverse[here, :] = inv
        normed[here, :] = (widened * inv * gain_ref[...]).astype(bf16)
        return carry

    lax.fori_loop(0, rows // group, normalise, 0, unroll=2)
    before = matmul(normed[...], down_ref[...], 1, 0)
    sig = jax.nn.sigmoid(before)
    active = (before * sig).astype(bf16)
    for k in range(column_groups):
        here = slice(k * span, (k + 1) * span)
        branch = matmul(active, up_ref[:, here], 1, 0)
        outputs = ((x_ref[:, here].astype(f32) + branch) * mask).astype(bf16)
        for g in range(rows // group):
            j, t = g // row_groups, g % row_groups
            src_f[t * column_groups + k, j] = outputs[g * group : (g + 1) * group]

    lane_rows = lax.broadcasted_iota(i32, tile_f.shape, 0)
    tile_f[...] = jnp.where(lane_rows == 0, route_fwd[0], route_fwd[1])
    tile_b[...] = jnp.where(lane_rows == 0, route_bwd[0], route_bwd[1])

    others = has_next.astype(i32) + has_prev.astype(i32) + 1
    pl.semaphore_wait(barrier, spread * others)

    def slots(origin):
        return pl.ds(1 + (c * spread + origin) * batches, batches)

    def spread_out(way, section, src, mid, tile, tiles):
        def tile_step(i, carry):
            pltpu.make_async_remote_copy(
                src_ref=tile, dst_ref=tiles.at[c, m],
                send_sem=tile_send.at[way], recv_sem=tile_recv.at[way],
                device_id=(section, 2 * partner(i) + c), device_id_type=MESH,
            ).start()
            return carry

        def step(i, carry):
            to = partner(i)
            pltpu.make_async_remote_copy(
                src_ref=src.at[to], dst_ref=mid.at[slots(m)],
                send_sem=p1_send.at[way], recv_sem=p1_recv.at[way, m],
                device_id=(section, 2 * to + c), device_id_type=MESH,
            ).start()
            return carry

        lax.fori_loop(0, spread, step, 0)
        lax.fori_loop(0, spread, tile_step, 0)

    @pl.when(has_next)
    def _():
        spread_out(0, s + 1, src_f, mid_f, tile_f, tiles_f)

    masked[...] = cot_ref[...] * mask_small
    act_grad = matmul(masked[...], up_ref[...], 1, 1)
    pre_grad = (act_grad * sig * (1.0 + before * (1.0 - sig))).astype(bf16)
    for k in range(column_groups):
        here = slice(k * span, (k + 1) * span)
        norm_grad[:, here] = matmul(pre_grad, down_ref[here, :], 1, 1)
    gain_acc[...] = jnp.zeros_like(gain_acc)

    def input_grad(g, carry):
        here = pl.ds(pl.multiple_of(g * group, group), group)
        inv = inverse[here, :]
        unit = x_ref[here, :].astype(f32) * inv
        ng = norm_grad[here, :]
        product = ng * unit
        gain_acc[...] += product[: group // 2] + product[group // 2 :]
        scaled = ng * gain_ref[...]
        mean = jnp.sum(scaled * unit, axis=-1, keepdims=True) / width
        grad = (masked[here, :].astype(f32) + inv * (scaled - unit * mean)).astype(bf16)
        for k in range(column_groups):
            src_b[(g % row_groups) * column_groups + k, g // row_groups] = grad[
                :, k * span : (k + 1) * span
            ]
        return carry

    lax.fori_loop(0, rows // group, input_grad, 0)

    @pl.when(has_prev)
    def _():
        spread_out(1, s - 1, src_b, mid_b, tile_b, tiles_b)

    per_group = span // share
    for k in range(column_groups):
        here = slice(k * span, (k + 1) * span)
        down_part = matmul(normed[:, here], pre_grad, 0, 0)
        up_part = matmul(masked[:, here], active, 0, 0)
        for i in range(per_group):
            q = k * per_group + i
            own = (q % 2, (q // 2) % 2, q // 4)
            mine = slice(i * share, (i + 1) * share)
            piece[own + (slice(0, share),)] = down_part[mine]
            piece[own + (slice(share, 2 * share),)] = up_part[mine]
            gains = gain_acc[:, q * share : (q + 1) * share]
            blank = jnp.zeros((gains.shape[0], units - share), f32)
            piece[own + (slice(2 * share, 2 * share + 8),)] = jnp.concatenate([gains, blank], axis=1)

    def to_core(k, half):
        return pltpu.make_async_remote_copy(
            src_ref=piece.at[1 - c, half], dst_ref=from_core.at[half],
            send_sem=core_send.at[k], recv_sem=core_recv.at[k],
            device_id=(s, sibling), device_id_type=MESH,
        )

    to_core(0, 1 - x).start()
    to_core(1, x).start()

    def add_core(k, half):
        arrived(from_core.at[half], core_recv.at[k])

        def step(i, carry):
            piece[c, half, i] += from_core[half, i]
            return carry

        lax.fori_loop(0, ring, step, 0)

    add_core(0, 1 - x)
    to_x = pltpu.make_async_remote_copy(
        src_ref=piece.at[c, 1 - x], dst_ref=from_x,
        send_sem=x_send, recv_sem=x_recv,
        device_id=(s, 2 * (m + 1 - 2 * x) + c), device_id_type=MESH,
    )
    to_x.start()
    add_core(1, x)

    def swap(way, mid, tiles):
        def step(i, carry):
            origin = partner(i)
            here = mid.at[slots(origin)]
            arrived(here, p1_recv.at[way, origin])
            pltpu.make_async_remote_copy(
                src_ref=here, dst_ref=here,
                send_sem=swap_send.at[way], recv_sem=swap_recv.at[way],
                device_id=(s, sibling), device_id_type=MESH,
            ).start()
            return carry

        lax.fori_loop(0, spread, step, 0)
        arrived(tiles.at[c], tile_recv.at[way])
        pltpu.make_async_remote_copy(
            src_ref=tiles.at[c], dst_ref=tiles.at[c],
            send_sem=tswap_send.at[way], recv_sem=tswap_recv.at[way],
            device_id=(s, sibling), device_id_type=MESH,
        ).start()

    def half_of(mid, core):
        return mid.at[pl.ds(1 + core * spread * batches, spread * batches)]

    def deliver(way, mid, tiles, table, pick, out):
        arrived(tiles.at[1 - c], tswap_recv.at[way])
        lanes = lax.broadcasted_iota(i32, (1, tiles.shape[3]), 1)

        def count(i, carry):
            seen, chosen = carry
            for core in range(2):
                for j in range(batches):
                    hit = tiles[core, i, j : j + 1, :] == lanes
                    name = 1 + (core * spread + i) * batches + j
                    chosen = tuple(
                        old + jnp.where(hit & (seen == k), name, 0) for k, old in enumerate(chosen)
                    )
                    seen = seen + hit.astype(i32)
            return seen, chosen

        table_v[...] = jnp.zeros_like(table_v)
        none = jnp.zeros_like(lanes)
        _, chosen = lax.fori_loop(0, spread, count, (none, (none,) * cap))
        for k in range(cap):
            table_v[k : k + 1, :] = chosen[k]
        to_table = pltpu.make_async_copy(table_v, table, table_sem.at[way])
        to_table.start()
        mid[0] = jnp.zeros(mid.shape[1:], bf16)
        to_table.wait()
        arrived(half_of(mid, 1 - c), swap_recv.at[way])

        tokens = pl.ds(pl.multiple_of((m // column_groups) * group, group), group)
        columns = pl.ds(pl.multiple_of((m % column_groups) * span, 128), span)

        def step(i, carry):
            to = partner(i)
            for k in range(cap):
                pick[to, k] = mid[table[k, 2 * to + c]]
            pltpu.make_async_remote_copy(
                src_ref=pick.at[to], dst_ref=out.at[:, tokens, columns],
                send_sem=p2_send.at[way], recv_sem=p2_recv.at[way],
                device_id=(s, 2 * to + c), device_id_type=MESH,
            ).start()
            return carry

        lax.fori_loop(1, spread, step, 0)
        for k in range(cap):
            out[k, tokens, columns] = mid[table[k, p]]

    def settle(way, mid, tiles, pick):
        arrived(pick.at[pl.ds(0, spread - 1)], p2_recv.at[way])
        arrived(pick.at[pl.ds(0, spread - 1)], p2_send.at[way])
        arrived(half_of(mid, c), swap_send.at[way])
        arrived(tiles.at[c], tswap_send.at[way])

    @pl.when(has_prev)
    def _():
        swap(0, mid_f, tiles_f)
        deliver(0, mid_f, tiles_f, table_f, pick_f, act_out)

    @pl.when(s == 0)
    def _():
        act_out[...] = jnp.zeros_like(act_out)

    turn = 1 - 2 * c
    far_a, far_b = ring // 2, ring - 1 - ring // 2

    def along(step):
        return (y + ring + step) % ring

    def chain_step(t, far, way, hold, send, recv):
        at = along(way * (far - t))
        if t > 0:
            arrived(hold.at[t - 1], recv.at[t - 1])
            piece[c, x, at] += hold[t - 1]
        pltpu.make_async_remote_copy(
            src_ref=piece.at[c, x, at], dst_ref=hold.at[t],
            send_sem=send.at[t], recv_sem=recv.at[t],
            device_id=(s, 4 * along(way) + 2 * x + c), device_id_type=MESH,
        ).start()

    arrived(from_x, x_recv)

    def add_x(i, carry):
        piece[c, x, i] += from_x[i]
        return carry

    lax.fori_loop(0, ring, add_x, 0)

    def both(t):
        if t < far_a:
            chain_step(t, far_a, turn, chain_a, a_send, a_recv)
        if t < far_b:
            chain_step(t, far_b, -turn, chain_b, b_send, b_recv)

    both(0)

    @pl.when(has_next)
    def _():
        swap(1, mid_b, tiles_b)

    for t in range(1, far_a):
        both(t)

    @pl.when(has_next)
    def _():
        deliver(1, mid_b, tiles_b, table_b, pick_b, grad_out)

    @pl.when(s == sections - 1)
    def _():
        grad_out[...] = jnp.zeros_like(grad_out)

    arrived(chain_a.at[far_a - 1], a_recv.at[far_a - 1])
    total = piece[c, x, y] + chain_a[far_a - 1]
    if far_b:
        arrived(chain_b.at[far_b - 1], b_recv.at[far_b - 1])
        total = total + chain_b[far_b - 1]
    total = total * (1.0 / peers)
    gdown_out[...] = total[:share]
    gup_out[...] = total[share : 2 * share].T
    ggain_out[...] = jnp.sum(total[2 * share :, :share], axis=0, keepdims=True)

    for k, half in enumerate((1 - x, x)):
        arrived(from_core.at[half], core_send.at[k])
    arrived(from_x, x_send)
    for t in range(far_a):
        arrived(chain_a.at[t], a_send.at[t])
    for t in range(far_b):
        arrived(chain_b.at[t], b_send.at[t])

    @pl.when(has_next)
    def _():
        arrived(src_f, p1_send.at[0])
        arrived(tiles_f.at[0], tile_send.at[0])

    @pl.when(has_prev)
    def _():
        arrived(src_b, p1_send.at[1])
        arrived(tiles_b.at[0], tile_send.at[1])

    @pl.when(has_prev)
    def _():
        settle(0, mid_f, tiles_f, pick_f)

    @pl.when(has_next)
    def _():
        settle(1, mid_b, tiles_b, pick_b)


def on_device(sections, peers, acts, cotangent, gain, w_down, w_up, route_fwd, route_bwd, token_counts):
    batches, length, width = acts.shape[2:]
    units = w_up.shape[1]
    cap = batches + batches // 2
    rows = batches * length
    spread = peers // 2
    ring = spread // 2
    group = 16
    span = width // (spread // (length // group))
    share = width // peers
    height = 2 * share + 8
    far_a, far_b = ring // 2, max(ring - 1 - ring // 2, 1)
    vmem, smem = pltpu.VMEM, pltpu.SMEM
    dma, pair = pltpu.SemaphoreType.DMA, pltpu.SemaphoreType.DMA((2,))
    in_vmem, in_smem = pl.BlockSpec(memory_space=vmem), pl.BlockSpec(memory_space=smem)
    mid = vmem((1 + 2 * spread * batches, group, span), bf16)
    pick = vmem((spread, cap, group, span), bf16)
    src = vmem((spread, batches, group, span), bf16)
    results = pl.pallas_call(
        functools.partial(kernel, sections, peers, cap),
        out_shape=(
            jax.ShapeDtypeStruct((cap, length, width), bf16),
            jax.ShapeDtypeStruct((cap, length, width), bf16),
            jax.ShapeDtypeStruct((share, units), f32),
            jax.ShapeDtypeStruct((units, share), f32),
            jax.ShapeDtypeStruct((1, share), f32),
        ),
        in_specs=[in_smem] * 3 + [in_vmem] * 5,
        out_specs=(in_vmem,) * 5,
        scratch_shapes=[
            vmem((rows, width), bf16),
            vmem((rows, width), bf16),
            vmem((rows, width), f32),
            vmem((rows, 1), f32),
            vmem((8, width), f32),
            src, src, mid, mid, pick, pick,
            vmem((8, 128), i32), vmem((8, 128), i32),
            vmem((2, spread, 8, 128), i32), vmem((2, spread, 8, 128), i32),
            vmem((8, 128), i32), smem((8, 128), i32), smem((8, 128), i32),
            vmem((2, 2, ring, height, units), f32),
            vmem((2, ring, height, units), f32),
            vmem((ring, height, units), f32),
            vmem((far_a, height, units), f32),
            vmem((far_b, height, units), f32),
            pair, dma((2, spread)), pair, pair, pair, pair,
            pair, pair, pair, pair, pair,
            pair, pair, dma, dma, dma((far_a,)), dma((far_a,)), dma((far_b,)), dma((far_b,)),
        ],
        compiler_params=pltpu.CompilerParams(
            collective_id=0, has_side_effects=True, vmem_limit_bytes=48 * 1024 * 1024
        ),
        cost_estimate=pl.CostEstimate(
            flops=12 * rows * width * units, bytes_accessed=8 * rows * width, transcendentals=rows * units
        ),
        name="adapter_relay",
    )(
        route_fwd.reshape(batches), route_bwd.reshape(batches), token_counts.reshape(batches),
        acts.reshape(rows, width), cotangent.reshape(rows, width), gain, w_down[0], w_up[0],
    )
    arrived_act, arrived_grad, grad_down, grad_up, grad_gain = results
    return arrived_act[None, None], arrived_grad[None, None], grad_down[None], grad_up[None], grad_gain


def solution(mesh):
    placed = (
        P("section", "peer", None, None, None),
        P("section", "peer", None, None, None),
        P("section", None),
        P("section", None, None),
        P("section", None, None),
        P("section", "peer", None),
        P("section", "peer", None),
        P("section", "peer", None),
    )
    return jax.shard_map(
        functools.partial(on_device, mesh.shape["section"], mesh.shape["peer"]),
        mesh=mesh,
        in_specs=placed,
        out_specs=(
            P("section", "peer", None, None, None),
            P("section", "peer", None, None, None),
            P("section", "peer", None),
            P("section", None, "peer"),
            P("section", "peer"),
        ),
        check_vma=False,
    )
```

time: 701 us -> 114 us (0.16)
  the two profiles are of different devices: /device:TPU:27 before, /device:TPU:20 now
where the time goes in v1:
time: 114 us; the launch traced here: 113 us
  Pallas kernels  104 us (91%)
  local copies, waits for them, and re-layouts  8.74 us (8%)
    pallas_call x1, Pallas kernels, on_device(): pl.pallas_call(functools.partial(kernel, sections, peers, cap), out_shape...  104 us
    unnamed x21, local copies, waits for them, and re-layouts  8.74 us

profile of v1, /device:TPU:20, one launch (start us, length us, event | category | flops | bytes accessed | tf_op | source)
XLA Modules:
  0.0 113.4 jit_solution(6743657634853175032)
XLA Ops:
  0.6 0.0 copy-start.4
  0.6 0.0 copy-start.5
  0.7 0.0 copy-start.6
  0.7 0.0 copy-start.7
  0.7 0.7 copy-done.4
  1.3 0.0 copy-done.5
  1.3 0.0 copy-done.6
  1.3 0.0 copy-done.7
  1.3 0.0 copy-start
  1.4 1.1 copy-done
  2.4 0.0 copy-start.1
  2.4 1.1 copy-done.1
  3.5 0.0 copy-start.2
  3.5 1.1 copy-done.2
  4.6 0.0 copy-start.3
  4.6 1.1 copy-done.3
  5.7 103.9 %adapter_relay.1 = (bf16[3,64,2560]{2,1,0:T(8,128)(2,1)S(1)}, bf16[3,64,2560]{2,1,0:T(8,128)(2,1)S(1)}, f32[80,128]{1,0:T(8,128)S(1)}, f32[128,80]{1,0:T(8,128)S(1)}, f32[1,80]{1,0:T(1,128)S(1)}) custom-call(s32[2]{0:T(128)S(1)} %bitcast.19, s32[2]{0:T(128)S(1)} %bitcast.20, s32[2]{0:T(128)S(1)} %bitcast.21, bf16[128,2560]{1,0:T(8,128)(2,1)S(1)} %bitcast.13, ...), custom_call_target="tpu_custom_call" | custom-call | flops 503316480 | bytes 2621440 | tf_op jit(solution)/shard_map/adapter_relay/pallas_call | solution.py:400
  109.6 0.7 copy.13
  110.3 0.9 copy.18
  111.3 0.9 copy.19
  112.2 0.6 copy.20
  112.8 0.5 copy.21
Async XLA Ops:
  0.6 0.7 copy-start.4
  0.6 0.7 copy-start.5
  0.7 0.7 copy-start.6
  0.7 0.7 copy-start.7
  1.3 1.1 copy-start
  2.4 1.1 copy-start.1
  3.5 1.1 copy-start.2
  4.6 1.1 copy-start.3

commit v2 on v1

--- a/solution.py
+++ b/solution.py
@@ -24,14 +24,16 @@
 
 def kernel(
     sections, peers, cap,
+    fwd_hbm, bwd_hbm, counts_hbm, x_hbm, cot_hbm, gain_hbm, down_hbm, up_hbm,
+    act_out, grad_out, gdown_out, gup_out, ggain_out,
     route_fwd, route_bwd, counts, x_ref, cot_ref, gain_ref, down_ref, up_ref,
-    act_out, grad_out, gdown_out, gup_out, ggain_out,
     normed, masked, norm_grad, inverse, gain_acc,
-    src_f, src_b, mid_f, mid_b, pick_f, pick_b,
-    tile_f, tile_b, tiles_f, tiles_b, table_v, table_f, table_b,
-    piece, from_core, from_x, chain_a, chain_b,
-    p1_send, p1_recv, swap_send, swap_recv, tile_send, tile_recv,
-    tswap_send, tswap_recv, table_sem, p2_send, p2_recv,
+    src_f, src_b, hop_f, hop_b, mid_f, mid_b, pick_f, pick_b,
+    tile, tiles_hop, tiles_f, tiles_b, table_v, table_f, table_b,
+    piece, from_core, from_x, chain_a, chain_b, final, final_gain,
+    hello, store_sem, load_sem, p1_send, p1_recv, z_send, z_recv, swap_send, swap_recv,
+    tile_send, tile_recv, tz_send, tz_recv, tswap_send, tswap_recv,
+    table_sem, p2_send, p2_recv,
     core_send, core_recv, x_send, x_recv, a_send, a_recv, b_send, b_recv,
 ):
     rows, width = x_ref.shape
@@ -50,6 +52,18 @@
     has_next = s < sections - 1
     has_prev = s > 0
 
+    loads = [
+        pltpu.make_async_copy(here, there, load_sem.at[k])
+        for k, (here, there) in enumerate(
+            (
+                (x_hbm, x_ref), (gain_hbm, gain_ref), (down_hbm, down_ref), (up_hbm, up_ref),
+                (counts_hbm, counts), (fwd_hbm, route_fwd), (bwd_hbm, route_bwd), (cot_hbm, cot_ref),
+            )
+        )
+    ]
+    for load in loads:
+        load.start()
+
     def partner(i):
         k = i // 2
         odd = k % 2
@@ -59,25 +73,18 @@
     barrier = pltpu.get_barrier_semaphore()
 
     def greet(i, carry):
-        q = 2 * partner(i) + c
-
-        @pl.when(has_next)
-        def _():
-            pl.semaphore_signal(barrier, inc=1, device_id=(s + 1, q), device_id_type=MESH)
-
-        @pl.when(has_prev)
-        def _():
-            pl.semaphore_signal(barrier, inc=1, device_id=(s - 1, q), device_id_type=MESH)
-
-        @pl.when(i > 0)
-        def _():
-            pl.semaphore_signal(barrier, inc=1, device_id=(s, q), device_id_type=MESH)
-
+        pl.semaphore_signal(barrier, inc=1, device_id=(s, 2 * partner(i) + c), device_id_type=MESH)
         return carry
 
-    lax.fori_loop(0, spread, greet, 0)
+    lax.fori_loop(1, spread, greet, 0)
     pl.semaphore_signal(barrier, inc=1, device_id=(s, sibling), device_id_type=MESH)
 
+    @pl.when(has_prev)
+    def _():
+        pl.semaphore_signal(barrier, inc=1, device_id=(s - 1, p), device_id_type=MESH)
+
+    for load in loads[:7]:
+        load.wait()
     row_ids = lax.broadcasted_iota(i32, (rows, 1), 0)
     limit = jnp.where(row_ids < length, counts[0], counts[1] + length)
     mask = (row_ids < limit).astype(f32)
@@ -103,41 +110,58 @@
             j, t = g // row_groups, g % row_groups
             src_f[t * column_groups + k, j] = outputs[g * group : (g + 1) * group]
 
-    lane_rows = lax.broadcasted_iota(i32, tile_f.shape, 0)
-    tile_f[...] = jnp.where(lane_rows == 0, route_fwd[0], route_fwd[1])
-    tile_b[...] = jnp.where(lane_rows == 0, route_bwd[0], route_bwd[1])
-
-    others = has_next.astype(i32) + has_prev.astype(i32) + 1
-    pl.semaphore_wait(barrier, spread * others)
+    kinds = lax.broadcasted_iota(i32, tile.shape, 0)
+    routes = jnp.where(
+        kinds < 2,
+        jnp.where(kinds == 0, route_fwd[0], route_fwd[1]),
+        jnp.where(kinds == 2, route_bwd[0], route_bwd[1]),
+    )
+    tile[...] = routes
+    tiles_hop[m] = routes
+
+    pl.semaphore_wait(barrier, spread + has_next.astype(i32))
+
+    @pl.when(has_next)
+    def _():
+        pl.semaphore_signal(hello, inc=1, device_id=(s + 1, p), device_id_type=MESH)
+
+    def send_tile(i, carry):
+        pltpu.make_async_remote_copy(
+            src_ref=tile, dst_ref=tiles_hop.at[m], send_sem=tile_send, recv_sem=tile_recv,
+            device_id=(s, 2 * partner(i) + c), device_id_type=MESH,
+        ).start()
+        return carry
+
+    lax.fori_loop(1, spread, send_tile, 0)
 
     def slots(origin):
         return pl.ds(1 + (c * spread + origin) * batches, batches)
 
-    def spread_out(way, section, src, mid, tile, tiles):
-        def tile_step(i, carry):
-            pltpu.make_async_remote_copy(
-                src_ref=tile, dst_ref=tiles.at[c, m],
-                send_sem=tile_send.at[way], recv_sem=tile_recv.at[way],
-                device_id=(section, 2 * partner(i) + c), device_id_type=MESH,
-            ).start()
-            return carry
-
+    def shift(way, chunk, origin, mid):
+        pltpu.make_async_remote_copy(
+            src_ref=chunk, dst_ref=mid.at[slots(origin)],
+            send_sem=z_send.at[way], recv_sem=z_recv.at[way, origin],
+            device_id=(s + 1 - 2 * way, p), device_id_type=MESH,
+        ).start()
+
+    def spread_out(way, src, hop):
         def step(i, carry):
             to = partner(i)
             pltpu.make_async_remote_copy(
-                src_ref=src.at[to], dst_ref=mid.at[slots(m)],
+                src_ref=src.at[to], dst_ref=hop.at[m],
                 send_sem=p1_send.at[way], recv_sem=p1_recv.at[way, m],
-                device_id=(section, 2 * to + c), device_id_type=MESH,
+                device_id=(s, 2 * to + c), device_id_type=MESH,
             ).start()
             return carry
 
-        lax.fori_loop(0, spread, step, 0)
-        lax.fori_loop(0, spread, tile_step, 0)
-
-    @pl.when(has_next)
-    def _():
-        spread_out(0, s + 1, src_f, mid_f, tile_f, tiles_f)
-
+        lax.fori_loop(1, spread, step, 0)
+
+    @pl.when(has_next)
+    def _():
+        spread_out(0, src_f, hop_f)
+        shift(0, src_f.at[m], m, mid_f)
+
+    loads[7].wait()
     masked[...] = cot_ref[...] * mask_small
     act_grad = matmul(masked[...], up_ref[...], 1, 1)
     pre_grad = (act_grad * sig * (1.0 + before * (1.0 - sig))).astype(bf16)
@@ -164,10 +188,6 @@
 
     lax.fori_loop(0, rows // group, input_grad, 0)
 
-    @pl.when(has_prev)
-    def _():
-        spread_out(1, s - 1, src_b, mid_b, tile_b, tiles_b)
-
     per_group = span // share
     for k in range(column_groups):
         here = slice(k * span, (k + 1) * span)
@@ -193,6 +213,10 @@
     to_core(0, 1 - x).start()
     to_core(1, x).start()
 
+    @pl.when(has_prev)
+    def _():
+        spread_out(1, src_b, hop_b)
+
     def add_core(k, half):
         arrived(from_core.at[half], core_recv.at[k])
 
@@ -211,11 +235,39 @@
     to_x.start()
     add_core(1, x)
 
+    arrived(tiles_hop.at[pl.ds(0, spread - 1)], tile_recv)
+
+    def shift_tiles(way, tiles):
+        pltpu.make_async_remote_copy(
+            src_ref=tiles_hop, dst_ref=tiles.at[c],
+            send_sem=tz_send.at[way], recv_sem=tz_recv.at[way],
+            device_id=(s + 1 - 2 * way, p), device_id_type=MESH,
+        ).start()
+
+    @pl.when(has_next)
+    def _():
+        shift_tiles(0, tiles_f)
+
+    @pl.when(has_prev)
+    def _():
+        pl.semaphore_wait(hello, 1)
+        shift_tiles(1, tiles_b)
+        shift(1, src_b.at[m], m, mid_b)
+
+    def relay(way, hop, mid, first, last):
+        def step(i, carry):
+            origin = partner(i)
+            arrived(hop.at[origin], p1_recv.at[way, origin])
+            shift(way, hop.at[origin], origin, mid)
+            return carry
+
+        lax.fori_loop(first, last, step, 0)
+
     def swap(way, mid, tiles):
         def step(i, carry):
             origin = partner(i)
             here = mid.at[slots(origin)]
-            arrived(here, p1_recv.at[way, origin])
+            arrived(here, z_recv.at[way, origin])
             pltpu.make_async_remote_copy(
                 src_ref=here, dst_ref=here,
                 send_sem=swap_send.at[way], recv_sem=swap_recv.at[way],
@@ -224,13 +276,21 @@
             return carry
 
         lax.fori_loop(0, spread, step, 0)
-        arrived(tiles.at[c], tile_recv.at[way])
+        arrived(tiles.at[c], tz_recv.at[way])
         pltpu.make_async_remote_copy(
             src_ref=tiles.at[c], dst_ref=tiles.at[c],
             send_sem=tswap_send.at[way], recv_sem=tswap_recv.at[way],
             device_id=(s, sibling), device_id_type=MESH,
         ).start()
 
+    def chunk_of(out, k):
+        tokens = pl.ds(pl.multiple_of((k // column_groups) * group, group), group)
+        columns = pl.ds(pl.multiple_of((k % column_groups) * span, 128), span)
+        return out.at[:, tokens, columns]
+
+    def keep(way, pick, out, k):
+        return pltpu.make_async_copy(pick.at[k], chunk_of(out, k), store_sem.at[way, k])
+
     def half_of(mid, core):
         return mid.at[pl.ds(1 + core * spread * batches, spread * batches)]
 
@@ -242,7 +302,8 @@
             seen, chosen = carry
             for core in range(2):
                 for j in range(batches):
-                    hit = tiles[core, i, j : j + 1, :] == lanes
+                    at = way * batches + j
+                    hit = tiles[core, i, at : at + 1, :] == lanes
                     name = 1 + (core * spread + i) * batches + j
                     chosen = tuple(
                         old + jnp.where(hit & (seen == k), name, 0) for k, old in enumerate(chosen)
@@ -261,15 +322,12 @@
         to_table.wait()
         arrived(half_of(mid, 1 - c), swap_recv.at[way])
 
-        tokens = pl.ds(pl.multiple_of((m // column_groups) * group, group), group)
-        columns = pl.ds(pl.multiple_of((m % column_groups) * span, 128), span)
-
         def step(i, carry):
             to = partner(i)
             for k in range(cap):
                 pick[to, k] = mid[table[k, 2 * to + c]]
             pltpu.make_async_remote_copy(
-                src_ref=pick.at[to], dst_ref=out.at[:, tokens, columns],
+                src_ref=pick.at[to], dst_ref=chunk_of(out, m),
                 send_sem=p2_send.at[way], recv_sem=p2_recv.at[way],
                 device_id=(s, 2 * to + c), device_id_type=MESH,
             ).start()
@@ -277,22 +335,21 @@
 
         lax.fori_loop(1, spread, step, 0)
         for k in range(cap):
-            out[k, tokens, columns] = mid[table[k, p]]
-
-    def settle(way, mid, tiles, pick):
-        arrived(pick.at[pl.ds(0, spread - 1)], p2_recv.at[way])
-        arrived(pick.at[pl.ds(0, spread - 1)], p2_send.at[way])
-        arrived(half_of(mid, c), swap_send.at[way])
-        arrived(tiles.at[c], tswap_send.at[way])
-
-    @pl.when(has_prev)
-    def _():
-        swap(0, mid_f, tiles_f)
-        deliver(0, mid_f, tiles_f, table_f, pick_f, act_out)
-
-    @pl.when(s == 0)
-    def _():
-        act_out[...] = jnp.zeros_like(act_out)
+            pick[m, k] = mid[table[k, p]]
+        keep(way, pick, out, m).start()
+
+    def clear(way, pick, out):
+        def fill(k, carry):
+            pick[k] = jnp.zeros(pick.shape[1:], bf16)
+            keep(way, pick, out, k).start()
+            return carry
+
+        def finish(k, carry):
+            keep(way, pick, out, k).wait()
+            return carry
+
+        lax.fori_loop(0, spread, fill, 0)
+        lax.fori_loop(0, spread, finish, 0)
 
     turn = 1 - 2 * c
     far_a, far_b = ring // 2, ring - 1 - ring // 2
@@ -311,28 +368,53 @@
             device_id=(s, 4 * along(way) + 2 * x + c), device_id_type=MESH,
         ).start()
 
-    arrived(from_x, x_recv)
-
-    def add_x(i, carry):
-        piece[c, x, i] += from_x[i]
-        return carry
-
-    lax.fori_loop(0, ring, add_x, 0)
-
-    def both(t):
+    def chains(t):
         if t < far_a:
             chain_step(t, far_a, turn, chain_a, a_send, a_recv)
         if t < far_b:
             chain_step(t, far_b, -turn, chain_b, b_send, b_recv)
 
-    both(0)
+    def add_x():
+        arrived(from_x, x_recv)
+
+        def step(i, carry):
+            piece[c, x, i] += from_x[i]
+            return carry
+
+        lax.fori_loop(0, ring, step, 0)
+
+    @pl.when(has_next)
+    def _():
+        relay(0, hop_f, mid_f, 1, spread)
+
+    @pl.when(has_prev)
+    def _():
+        relay(1, hop_b, mid_b, 1, spread)
+
+    add_x()
+    chains(0)
+
+    @pl.when(has_prev)
+    def _():
+        swap(0, mid_f, tiles_f)
+
+    chains(1)
+
+    @pl.when(has_prev)
+    def _():
+        deliver(0, mid_f, tiles_f, table_f, pick_f, act_out)
+
+    @pl.when(s == 0)
+    def _():
+        clear(0, pick_f, act_out)
+
+    chains(2)
 
     @pl.when(has_next)
     def _():
         swap(1, mid_b, tiles_b)
 
-    for t in range(1, far_a):
-        both(t)
+    chains(3)
 
     @pl.when(has_next)
     def _():
@@ -340,7 +422,8 @@
 
     @pl.when(s == sections - 1)
     def _():
-        grad_out[...] = jnp.zeros_like(grad_out)
+        clear(1, pick_b, grad_out)
+
 
     arrived(chain_a.at[far_a - 1], a_recv.at[far_a - 1])
     total = piece[c, x, y] + chain_a[far_a - 1]
@@ -348,9 +431,15 @@
         arrived(chain_b.at[far_b - 1], b_recv.at[far_b - 1])
         total = total + chain_b[far_b - 1]
     total = total * (1.0 / peers)
-    gdown_out[...] = total[:share]
-    gup_out[...] = total[share : 2 * share].T
-    ggain_out[...] = jnp.sum(total[2 * share :, :share], axis=0, keepdims=True)
+    final[...] = total
+    final_gain[...] = jnp.sum(total[2 * share :, :share], axis=0, keepdims=True)
+    stores = (
+        pltpu.make_async_copy(final.at[pl.ds(0, share)], gdown_out, load_sem.at[0]),
+        pltpu.make_async_copy(final.at[pl.ds(share, share)], gup_out, load_sem.at[1]),
+        pltpu.make_async_copy(final_gain, ggain_out, load_sem.at[2]),
+    )
+    for store in stores:
+        store.start()
 
     for k, half in enumerate((1 - x, x)):
         arrived(from_core.at[half], core_send.at[k])
@@ -359,24 +448,53 @@
         arrived(chain_a.at[t], a_send.at[t])
     for t in range(far_b):
         arrived(chain_b.at[t], b_send.at[t])
-
-    @pl.when(has_next)
-    def _():
-        arrived(src_f, p1_send.at[0])
-        arrived(tiles_f.at[0], tile_send.at[0])
-
-    @pl.when(has_prev)
-    def _():
-        arrived(src_b, p1_send.at[1])
-        arrived(tiles_b.at[0], tile_send.at[1])
-
-    @pl.when(has_prev)
-    def _():
-        settle(0, mid_f, tiles_f, pick_f)
-
-    @pl.when(has_next)
-    def _():
-        settle(1, mid_b, tiles_b, pick_b)
+    arrived(tiles_hop.at[pl.ds(0, spread - 1)], tile_send)
+
+    for store in stores:
+        store.wait()
+
+    def settle_out(way, src):
+        arrived(src.at[pl.ds(0, spread - 1)], p1_send.at[way])
+        arrived(src, z_send.at[way])
+        arrived(tiles_hop, tz_send.at[way])
+
+    def settle_in(way, mid, tiles, pick, out):
+        keep(way, pick, out, m).wait()
+        arrived(half_of(mid, c), swap_send.at[way])
+        arrived(tiles.at[c], tswap_send.at[way])
+        arrived(pick.at[pl.ds(0, spread - 1)], p2_send.at[way])
+        arrived(pick.at[pl.ds(0, spread - 1)], p2_recv.at[way])
+
+    @pl.when(has_next)
+    def _():
+        settle_out(0, src_f)
+
+    @pl.when(has_prev)
+    def _():
+        settle_out(1, src_b)
+
+    @pl.when(has_prev)
+    def _():
+        settle_in(0, mid_f, tiles_f, pick_f, act_out)
+
+    @pl.when(has_next)
+    def _():
+        settle_in(1, mid_b, tiles_b, pick_b, grad_out)
+
+
+def place(*refs):
+    count = (len(refs) - 2) // 3
+    given, results, held = (refs[k * count : (k + 1) * count] for k in range(3))
+    load_sem, store_sem = refs[-2:]
+    loads = [pltpu.make_async_copy(given[k], held[k], load_sem.at[k]) for k in range(count)]
+    stores = [pltpu.make_async_copy(held[k], results[k], store_sem.at[k]) for k in range(count)]
+    for load in loads:
+        load.start()
+    for load, store in zip(loads, stores):
+        load.wait()
+        store.start()
+    for store in stores:
+        store.wait()
 
 
 def on_device(sections, peers, acts, cotangent, gain, w_down, w_up, route_fwd, route_bwd, token_counts):
@@ -393,29 +511,33 @@
     far_a, far_b = ring // 2, max(ring - 1 - ring // 2, 1)
     vmem, smem = pltpu.VMEM, pltpu.SMEM
     dma, pair = pltpu.SemaphoreType.DMA, pltpu.SemaphoreType.DMA((2,))
-    in_vmem, in_smem = pl.BlockSpec(memory_space=vmem), pl.BlockSpec(memory_space=smem)
+    in_hbm = pl.BlockSpec(memory_space=pltpu.HBM)
     mid = vmem((1 + 2 * spread * batches, group, span), bf16)
     pick = vmem((spread, cap, group, span), bf16)
     src = vmem((spread, batches, group, span), bf16)
+    shapes = (
+        jax.ShapeDtypeStruct((cap, length, width), bf16),
+        jax.ShapeDtypeStruct((cap, length, width), bf16),
+        jax.ShapeDtypeStruct((share, units), f32),
+        jax.ShapeDtypeStruct((share, units), f32),
+        jax.ShapeDtypeStruct((1, share), f32),
+    )
     results = pl.pallas_call(
         functools.partial(kernel, sections, peers, cap),
-        out_shape=(
-            jax.ShapeDtypeStruct((cap, length, width), bf16),
-            jax.ShapeDtypeStruct((cap, length, width), bf16),
-            jax.ShapeDtypeStruct((share, units), f32),
-            jax.ShapeDtypeStruct((units, share), f32),
-            jax.ShapeDtypeStruct((1, share), f32),
-        ),
-        in_specs=[in_smem] * 3 + [in_vmem] * 5,
-        out_specs=(in_vmem,) * 5,
+        out_shape=shapes,
+        in_specs=[in_hbm] * 8,
+        out_specs=(in_hbm,) * 5,
         scratch_shapes=[
+            smem((batches,), i32), smem((batches,), i32), smem((batches,), i32),
+            vmem((rows, width), bf16), vmem((rows, width), bf16), vmem((1, width), f32),
+            vmem((width, units), bf16), vmem((units, width), bf16),
             vmem((rows, width), bf16),
             vmem((rows, width), bf16),
             vmem((rows, width), f32),
             vmem((rows, 1), f32),
             vmem((8, width), f32),
-            src, src, mid, mid, pick, pick,
-            vmem((8, 128), i32), vmem((8, 128), i32),
+            src, src, src, src, mid, mid, pick, pick,
+            vmem((8, 128), i32), vmem((spread, 8, 128), i32),
             vmem((2, spread, 8, 128), i32), vmem((2, spread, 8, 128), i32),
             vmem((8, 128), i32), smem((8, 128), i32), smem((8, 128), i32),
             vmem((2, 2, ring, height, units), f32),
@@ -423,12 +545,14 @@
             vmem((ring, height, units), f32),
             vmem((far_a, height, units), f32),
             vmem((far_b, height, units), f32),
-            pair, dma((2, spread)), pair, pair, pair, pair,
-            pair, pair, pair, pair, pair,
+            vmem((height, units), f32), vmem((1, share), f32),
+            pltpu.SemaphoreType.REGULAR, dma((2, spread)), dma((8,)), pair, dma((2, spread)), pair, dma((2, spread)), pair, pair,
+            dma, dma, pair, pair, pair, pair,
+            pair, pair, pair,
             pair, pair, dma, dma, dma((far_a,)), dma((far_a,)), dma((far_b,)), dma((far_b,)),
         ],
         compiler_params=pltpu.CompilerParams(
-            collective_id=0, has_side_effects=True, vmem_limit_bytes=48 * 1024 * 1024
+            collective_id=0, has_side_effects=True, vmem_limit_bytes=60 * 1024 * 1024
         ),
         cost_estimate=pl.CostEstimate(
             flops=12 * rows * width * units, bytes_accessed=8 * rows * width, transcendentals=rows * units
@@ -438,8 +562,16 @@
         route_fwd.reshape(batches), route_bwd.reshape(batches), token_counts.reshape(batches),
         acts.reshape(rows, width), cotangent.reshape(rows, width), gain, w_down[0], w_up[0],
     )
-    arrived_act, arrived_grad, grad_down, grad_up, grad_gain = results
-    return arrived_act[None, None], arrived_grad[None, None], grad_down[None], grad_up[None], grad_gain
+    arrived_act, arrived_grad, grad_down, grad_up, grad_gain = pl.pallas_call(
+        place,
+        out_shape=shapes,
+        in_specs=[in_hbm] * 5,
+        out_specs=(in_hbm,) * 5,
+        scratch_shapes=[vmem(made.shape, made.dtype) for made in shapes] + [dma((5,)), dma((5,))],
+        compiler_params=pltpu.CompilerParams(vmem_limit_bytes=60 * 1024 * 1024),
+        name="place_results",
+    )(*results)
+    return arrived_act[None, None], arrived_grad[None, None], grad_down[None], grad_up.T[None], grad_gain
 
 
 def solution(mesh):

time: 114 us -> 99.8 us (0.88)
  the two profiles are of different devices: /device:TPU:20 before, /device:TPU:196 now
where the time goes in v2:
time: 99.8 us; the launch traced here: 99.6 us
  Pallas kernels  99 us (99%)
    pallas_call x1, Pallas kernels, on_device(): pl.pallas_call(functools.partial(kernel, sections, peers, cap), out_shape...  96.4 us
    pallas_call x1, Pallas kernels, on_device(): pl.pallas_call(place, out_shape=shapes, in_specs=[in_hbm] * 5, out_specs=...  2.57 us

profile of v2, /device:TPU:196, one launch (start us, length us, event | category | flops | bytes accessed | tf_op | source)
XLA Modules:
  0.0 99.6 jit_solution(7451375885550622208)
XLA Ops:
  0.6 96.4 %adapter_relay.1 = (bf16[3,64,2560]{2,1,0:T(8,128)(2,1)}, bf16[3,64,2560]{2,1,0:T(8,128)(2,1)}, f32[80,128]{1,0:T(8,128)}, f32[80,128]{1,0:T(8,128)}, f32[1,80]{1,0:T(1,128)}) custom-call(s32[2]{0:T(128)} %bitcast.17, s32[2]{0:T(128)} %bitcast.18, s32[2]{0:T(128)} %bitcast.19, bf16[128,2560]{1,0:T(8,128)(2,1)} %bitcast.13, bf16[128,2560]{1,0:T(8,128)(2,1)} %bitcast.14, ...), custom_call_target="tpu_custom_call" | custom-call | flops 503316480 | bytes 2621440 | tf_op jit(solution)/shard_map/adapter_relay/pallas_call | solution.py:525
  97.0 2.6 %place_results.1 = (bf16[3,64,2560]{2,1,0:T(8,128)(2,1)}, bf16[3,64,2560]{2,1,0:T(8,128)(2,1)}, f32[80,128]{1,0:T(8,128)}, f32[80,128]{1,0:T(8,128)}, f32[1,80]{1,0:T(1,128)}) custom-call(bf16[3,64,2560]{2,1,0:T(8,128)(2,1)} %get-tuple-element.15.refs_0_, bf16[3,64,2560]{2,1,0:T(8,128)(2,1)} %get-tuple-element.16.refs_1_, ...), custom_call_target="tpu_custom_call" | custom-call | tf_op jit(solution)/shard_map/place_results/pallas_call | solution.py:565

commit v3 on v2

--- a/solution.py
+++ b/solution.py
@@ -30,7 +30,7 @@
     normed, masked, norm_grad, inverse, gain_acc,
     src_f, src_b, hop_f, hop_b, mid_f, mid_b, pick_f, pick_b,
     tile, tiles_hop, tiles_f, tiles_b, table_v, table_f, table_b,
-    piece, from_core, from_x, chain_a, chain_b, final, final_gain,
+    piece, from_core, sum_x, from_x, part_a, part_b, chain_a, chain_b, final, final_gain,
     hello, store_sem, load_sem, p1_send, p1_recv, z_send, z_recv, swap_send, swap_recv,
     tile_send, tile_recv, tz_send, tz_recv, tswap_send, tswap_recv,
     table_sem, p2_send, p2_recv,
@@ -156,6 +156,15 @@
 
         lax.fori_loop(1, spread, step, 0)
 
+    def relay(way, hop, mid, first, last):
+        def step(i, carry):
+            origin = partner(i)
+            arrived(hop.at[origin], p1_recv.at[way, origin])
+            shift(way, hop.at[origin], origin, mid)
+            return carry
+
+        lax.fori_loop(first, last, step, 0)
+
     @pl.when(has_next)
     def _():
         spread_out(0, src_f, hop_f)
@@ -176,7 +185,7 @@
         unit = x_ref[here, :].astype(f32) * inv
         ng = norm_grad[here, :]
         product = ng * unit
-        gain_acc[...] += product[: group // 2] + product[group // 2 :]
+        gain_acc[...] += product
         scaled = ng * gain_ref[...]
         mean = jnp.sum(scaled * unit, axis=-1, keepdims=True) / width
         grad = (masked[here, :].astype(f32) + inv * (scaled - unit * mean)).astype(bf16)
@@ -201,7 +210,7 @@
             piece[own + (slice(share, 2 * share),)] = up_part[mine]
             gains = gain_acc[:, q * share : (q + 1) * share]
             blank = jnp.zeros((gains.shape[0], units - share), f32)
-            piece[own + (slice(2 * share, 2 * share + 8),)] = jnp.concatenate([gains, blank], axis=1)
+            piece[own + (slice(2 * share, 2 * share + group),)] = jnp.concatenate([gains, blank], axis=1)
 
     def to_core(k, half):
         return pltpu.make_async_remote_copy(
@@ -217,18 +226,26 @@
     def _():
         spread_out(1, src_b, hop_b)
 
+    @pl.when(has_next)
+    def _():
+        relay(0, hop_f, mid_f, 1, 8)
+
     def add_core(k, half):
         arrived(from_core.at[half], core_recv.at[k])
 
         def step(i, carry):
-            piece[c, half, i] += from_core[half, i]
+            total = piece[c, half, i] + from_core[half, i]
+            if k == 0:
+                sum_x[i] = total.astype(bf16)
+            else:
+                piece[c, half, i] = total
             return carry
 
         lax.fori_loop(0, ring, step, 0)
 
     add_core(0, 1 - x)
     to_x = pltpu.make_async_remote_copy(
-        src_ref=piece.at[c, 1 - x], dst_ref=from_x,
+        src_ref=sum_x, dst_ref=from_x,
         send_sem=x_send, recv_sem=x_recv,
         device_id=(s, 2 * (m + 1 - 2 * x) + c), device_id_type=MESH,
     )
@@ -253,15 +270,6 @@
         pl.semaphore_wait(hello, 1)
         shift_tiles(1, tiles_b)
         shift(1, src_b.at[m], m, mid_b)
-
-    def relay(way, hop, mid, first, last):
-        def step(i, carry):
-            origin = partner(i)
-            arrived(hop.at[origin], p1_recv.at[way, origin])
-            shift(way, hop.at[origin], origin, mid)
-            return carry
-
-        lax.fori_loop(first, last, step, 0)
 
     def swap(way, mid, tiles):
         def step(i, carry):
@@ -294,7 +302,7 @@
     def half_of(mid, core):
         return mid.at[pl.ds(1 + core * spread * batches, spread * batches)]
 
-    def deliver(way, mid, tiles, table, pick, out):
+    def look_up(way, mid, tiles, table):
         arrived(tiles.at[1 - c], tswap_recv.at[way])
         lanes = lax.broadcasted_iota(i32, (1, tiles.shape[3]), 1)
 
@@ -322,6 +330,7 @@
         to_table.wait()
         arrived(half_of(mid, 1 - c), swap_recv.at[way])
 
+    def deliver(way, mid, table, pick, out, first, last):
         def step(i, carry):
             to = partner(i)
             for k in range(cap):
@@ -333,7 +342,9 @@
             ).start()
             return carry
 
-        lax.fori_loop(1, spread, step, 0)
+        lax.fori_loop(first, last, step, 0)
+
+    def deliver_own(way, mid, table, pick, out):
         for k in range(cap):
             pick[m, k] = mid[table[k, p]]
         keep(way, pick, out, m).start()
@@ -357,68 +368,88 @@
     def along(step):
         return (y + ring + step) % ring
 
-    def chain_step(t, far, way, hold, send, recv):
-        at = along(way * (far - t))
+    def chain_step(t, far, way, part, hold, send, recv):
+        total = piece[c, x, along(way * (far - t))]
         if t > 0:
             arrived(hold.at[t - 1], recv.at[t - 1])
-            piece[c, x, at] += hold[t - 1]
+            total = total + hold[t - 1].astype(f32)
+        part[t] = total.astype(bf16)
         pltpu.make_async_remote_copy(
-            src_ref=piece.at[c, x, at], dst_ref=hold.at[t],
+            src_ref=part.at[t], dst_ref=hold.at[t],
             send_sem=send.at[t], recv_sem=recv.at[t],
             device_id=(s, 4 * along(way) + 2 * x + c), device_id_type=MESH,
         ).start()
 
     def chains(t):
         if t < far_a:
-            chain_step(t, far_a, turn, chain_a, a_send, a_recv)
+            chain_step(t, far_a, turn, part_a, chain_a, a_send, a_recv)
         if t < far_b:
-            chain_step(t, far_b, -turn, chain_b, b_send, b_recv)
+            chain_step(t, far_b, -turn, part_b, chain_b, b_send, b_recv)
 
     def add_x():
         arrived(from_x, x_recv)
 
         def step(i, carry):
-            piece[c, x, i] += from_x[i]
+            piece[c, x, i] += from_x[i].astype(f32)
             return carry
 
         lax.fori_loop(0, ring, step, 0)
 
     @pl.when(has_next)
     def _():
-        relay(0, hop_f, mid_f, 1, spread)
-
-    @pl.when(has_prev)
-    def _():
-        relay(1, hop_b, mid_b, 1, spread)
+        relay(0, hop_f, mid_f, 8, spread)
+
+    @pl.when(has_prev)
+    def _():
+        swap(0, mid_f, tiles_f)
 
     add_x()
     chains(0)
 
     @pl.when(has_prev)
     def _():
-        swap(0, mid_f, tiles_f)
+        look_up(0, mid_f, tiles_f, table_f)
+        deliver(0, mid_f, table_f, pick_f, act_out, 1, spread)
+        deliver_own(0, mid_f, table_f, pick_f, act_out)
+
+    @pl.when(s == 0)
+    def _():
+        clear(0, pick_f, act_out)
+
+    @pl.when(has_prev)
+    def _():
+        relay(1, hop_b, mid_b, 1, spread)
+
+    @pl.when(has_next)
+    def _():
+        swap(1, mid_b, tiles_b)
+
+    @pl.when(has_next)
+    def _():
+        look_up(1, mid_b, tiles_b, table_b)
+        deliver_own(1, mid_b, table_b, pick_b, grad_out)
+
+    @pl.when(has_next)
+    def _():
+        deliver(1, mid_b, table_b, pick_b, grad_out, 1, 5)
 
     chains(1)
 
-    @pl.when(has_prev)
-    def _():
-        deliver(0, mid_f, tiles_f, table_f, pick_f, act_out)
-
-    @pl.when(s == 0)
-    def _():
-        clear(0, pick_f, act_out)
+    @pl.when(has_next)
+    def _():
+        deliver(1, mid_b, table_b, pick_b, grad_out, 5, 9)
 
     chains(2)
 
     @pl.when(has_next)
     def _():
-        swap(1, mid_b, tiles_b)
+        deliver(1, mid_b, table_b, pick_b, grad_out, 9, 13)
 
     chains(3)
 
     @pl.when(has_next)
     def _():
-        deliver(1, mid_b, tiles_b, table_b, pick_b, grad_out)
+        deliver(1, mid_b, table_b, pick_b, grad_out, 13, 16)
 
     @pl.when(s == sections - 1)
     def _():
@@ -426,10 +457,10 @@
 
 
     arrived(chain_a.at[far_a - 1], a_recv.at[far_a - 1])
-    total = piece[c, x, y] + chain_a[far_a - 1]
+    total = piece[c, x, y] + chain_a[far_a - 1].astype(f32)
     if far_b:
         arrived(chain_b.at[far_b - 1], b_recv.at[far_b - 1])
-        total = total + chain_b[far_b - 1]
+        total = total + chain_b[far_b - 1].astype(f32)
     total = total * (1.0 / peers)
     final[...] = total
     final_gain[...] = jnp.sum(total[2 * share :, :share], axis=0, keepdims=True)
@@ -507,7 +538,7 @@
     group = 16
     span = width // (spread // (length // group))
     share = width // peers
-    height = 2 * share + 8
+    height = 2 * share + group
     far_a, far_b = ring // 2, max(ring - 1 - ring // 2, 1)
     vmem, smem = pltpu.VMEM, pltpu.SMEM
     dma, pair = pltpu.SemaphoreType.DMA, pltpu.SemaphoreType.DMA((2,))
@@ -535,16 +566,16 @@
             vmem((rows, width), bf16),
             vmem((rows, width), f32),
             vmem((rows, 1), f32),
-            vmem((8, width), f32),
+            vmem((group, width), f32),
             src, src, src, src, mid, mid, pick, pick,
             vmem((8, 128), i32), vmem((spread, 8, 128), i32),
             vmem((2, spread, 8, 128), i32), vmem((2, spread, 8, 128), i32),
             vmem((8, 128), i32), smem((8, 128), i32), smem((8, 128), i32),
             vmem((2, 2, ring, height, units), f32),
             vmem((2, ring, height, units), f32),
-            vmem((ring, height, units), f32),
-            vmem((far_a, height, units), f32),
-            vmem((far_b, height, units), f32),
+            vmem((ring, height, units), bf16), vmem((ring, height, units), bf16),
+            vmem((far_a, height, units), bf16), vmem((far_b, height, units), bf16),
+            vmem((far_a, height, units), bf16), vmem((far_b, height, units), bf16),
             vmem((height, units), f32), vmem((1, share), f32),
             pltpu.SemaphoreType.REGULAR, dma((2, spread)), dma((8,)), pair, dma((2, spread)), pair, dma((2, spread)), pair, pair,
             dma, dma, pair, pair, pair, pair,

time: 99.8 us -> 95.6 us (0.958)
  the two profiles are of different devices: /device:TPU:196 before, /device:TPU:13 now
where the time goes in v3:
time: 95.6 us; the launch traced here: 95.5 us
  Pallas kernels  94.8 us (99%)
    pallas_call x1, Pallas kernels, on_device(): pl.pallas_call(functools.partial(kernel, sections, peers, cap), out_shape...  92.2 us
    pallas_call x1, Pallas kernels, on_device(): pl.pallas_call(place, out_shape=shapes, in_specs=[in_hbm] * 5, out_specs=...  2.57 us

profile of v3, /device:TPU:13, one launch (start us, length us, event | category | flops | bytes accessed | tf_op | source)
XLA Modules:
  0.0 95.5 jit_solution(16215544153494837091)
XLA Ops:
  0.6 92.2 %adapter_relay.1 = (bf16[3,64,2560]{2,1,0:T(8,128)(2,1)}, bf16[3,64,2560]{2,1,0:T(8,128)(2,1)}, f32[80,128]{1,0:T(8,128)}, f32[80,128]{1,0:T(8,128)}, f32[1,80]{1,0:T(1,128)}) custom-call(s32[2]{0:T(128)} %bitcast.17, s32[2]{0:T(128)} %bitcast.18, s32[2]{0:T(128)} %bitcast.19, bf16[128,2560]{1,0:T(8,128)(2,1)} %bitcast.13, bf16[128,2560]{1,0:T(8,128)(2,1)} %bitcast.14, ...), custom_call_target="tpu_custom_call" | custom-call | flops 503316480 | bytes 2621440 | tf_op jit(solution)/shard_map/adapter_relay/pallas_call | solution.py:556
  92.9 2.6 %place_results.1 = (bf16[3,64,2560]{2,1,0:T(8,128)(2,1)}, bf16[3,64,2560]{2,1,0:T(8,128)(2,1)}, f32[80,128]{1,0:T(8,128)}, f32[80,128]{1,0:T(8,128)}, f32[1,80]{1,0:T(1,128)}) custom-call(bf16[3,64,2560]{2,1,0:T(8,128)(2,1)} %get-tuple-element.15.refs_0_, bf16[3,64,2560]{2,1,0:T(8,128)(2,1)} %get-tuple-element.16.refs_1_, ...), custom_call_target="tpu_custom_call" | custom-call | tf_op jit(solution)/shard_map/place_results/pallas_call | solution.py:596

commit v4 on v3

--- a/solution.py
+++ b/solution.py
@@ -222,13 +222,13 @@
     to_core(0, 1 - x).start()
     to_core(1, x).start()
 
+    @pl.when(has_next)
+    def _():
+        relay(0, hop_f, mid_f, 1, spread // 2)
+
     @pl.when(has_prev)
     def _():
         spread_out(1, src_b, hop_b)
-
-    @pl.when(has_next)
-    def _():
-        relay(0, hop_f, mid_f, 1, 8)
 
     def add_core(k, half):
         arrived(from_core.at[half], core_recv.at[k])
@@ -332,7 +332,7 @@
 
     def deliver(way, mid, table, pick, out, first, last):
         def step(i, carry):
-            to = partner(i)
+            to = partner(spread - i)
             for k in range(cap):
                 pick[to, k] = mid[table[k, 2 * to + c]]
             pltpu.make_async_remote_copy(
@@ -395,9 +395,11 @@
 
         lax.fori_loop(0, ring, step, 0)
 
-    @pl.when(has_next)
-    def _():
-        relay(0, hop_f, mid_f, 8, spread)
+    quarter = spread // 4
+
+    @pl.when(has_next)
+    def _():
+        relay(0, hop_f, mid_f, spread // 2, spread)
 
     @pl.when(has_prev)
     def _():
@@ -431,25 +433,25 @@
 
     @pl.when(has_next)
     def _():
-        deliver(1, mid_b, table_b, pick_b, grad_out, 1, 5)
+        deliver(1, mid_b, table_b, pick_b, grad_out, 1, 1 + quarter)
 
     chains(1)
 
     @pl.when(has_next)
     def _():
-        deliver(1, mid_b, table_b, pick_b, grad_out, 5, 9)
+        deliver(1, mid_b, table_b, pick_b, grad_out, 1 + quarter, 1 + 2 * quarter)
 
     chains(2)
 
     @pl.when(has_next)
     def _():
-        deliver(1, mid_b, table_b, pick_b, grad_out, 9, 13)
+        deliver(1, mid_b, table_b, pick_b, grad_out, 1 + 2 * quarter, 1 + 3 * quarter)
 
     chains(3)
 
     @pl.when(has_next)
     def _():
-        deliver(1, mid_b, table_b, pick_b, grad_out, 13, 16)
+        deliver(1, mid_b, table_b, pick_b, grad_out, 1 + 3 * quarter, spread)
 
     @pl.when(s == sections - 1)
     def _():
@@ -517,8 +519,13 @@
     count = (len(refs) - 2) // 3
     given, results, held = (refs[k * count : (k + 1) * count] for k in range(3))
     load_sem, store_sem = refs[-2:]
-    loads = [pltpu.make_async_copy(given[k], held[k], load_sem.at[k]) for k in range(count)]
-    stores = [pltpu.make_async_copy(held[k], results[k], store_sem.at[k]) for k in range(count)]
+    slots = given[0].shape[0]
+    parts = [(k, pl.ds(i, 1)) for i in range(slots) for k in (0, 1)]
+    parts += [(k, slice(None)) for k in range(2, count)]
+    loads, stores = [], []
+    for n, (k, cut) in enumerate(parts):
+        loads.append(pltpu.make_async_copy(given[k].at[cut], held[k].at[cut], load_sem.at[n]))
+        stores.append(pltpu.make_async_copy(held[k].at[cut], results[k].at[cut], store_sem.at[n]))
     for load in loads:
         load.start()
     for load, store in zip(loads, stores):
@@ -598,7 +605,7 @@
         out_shape=shapes,
         in_specs=[in_hbm] * 5,
         out_specs=(in_hbm,) * 5,
-        scratch_shapes=[vmem(made.shape, made.dtype) for made in shapes] + [dma((5,)), dma((5,))],
+        scratch_shapes=[vmem(made.shape, made.dtype) for made in shapes] + [dma((2 * cap + 3,)), dma((2 * cap + 3,))],
         compiler_params=pltpu.CompilerParams(vmem_limit_bytes=60 * 1024 * 1024),
         name="place_results",
     )(*results)

time: 95.6 us -> 93.8 us (0.981)
  the two profiles are of different devices: /device:TPU:13 before, /device:TPU:7 now
where the time goes in v4:
time: 93.8 us; the launch traced here: 93 us
  Pallas kernels  92.3 us (98%)
    pallas_call x1, Pallas kernels, on_device(): pl.pallas_call(functools.partial(kernel, sections, peers, cap), out_shape...  89.9 us
    pallas_call x1, Pallas kernels, on_device(): pl.pallas_call(place, out_shape=shapes, in_specs=[in_hbm] * 5, out_specs=...  2.41 us

profile of v4, /device:TPU:7, one launch (start us, length us, event | category | flops | bytes accessed | tf_op | source)
XLA Modules:
  0.0 93.0 jit_solution(6792116429725260114)
XLA Ops:
  0.6 89.9 %adapter_relay.1 = (bf16[3,64,2560]{2,1,0:T(8,128)(2,1)}, bf16[3,64,2560]{2,1,0:T(8,128)(2,1)}, f32[80,128]{1,0:T(8,128)}, f32[80,128]{1,0:T(8,128)}, f32[1,80]{1,0:T(1,128)}) custom-call(s32[2]{0:T(128)} %bitcast.17, s32[2]{0:T(128)} %bitcast.18, s32[2]{0:T(128)} %bitcast.19, bf16[128,2560]{1,0:T(8,128)(2,1)} %bitcast.13, bf16[128,2560]{1,0:T(8,128)(2,1)} %bitcast.14, ...), custom_call_target="tpu_custom_call" | custom-call | flops 503316480 | bytes 2621440 | tf_op jit(solution)/shard_map/adapter_relay/pallas_call | solution.py:563
  90.6 2.4 %place_results.1 = (bf16[3,64,2560]{2,1,0:T(8,128)(2,1)}, bf16[3,64,2560]{2,1,0:T(8,128)(2,1)}, f32[80,128]{1,0:T(8,128)}, f32[80,128]{1,0:T(8,128)}, f32[1,80]{1,0:T(1,128)}) custom-call(bf16[3,64,2560]{2,1,0:T(8,128)(2,1)} %get-tuple-element.15.refs_0_, bf16[3,64,2560]{2,1,0:T(8,128)(2,1)} %get-tuple-element.16.refs_1_, ...), custom_call_target="tpu_custom_call" | custom-call | tf_op jit(solution)/shard_map/place_results/pallas_call | solution.py:603

commit v5 on v4

--- a/solution.py
+++ b/solution.py
@@ -426,6 +426,8 @@
     def _():
         swap(1, mid_b, tiles_b)
 
+    chains(1)
+
     @pl.when(has_next)
     def _():
         look_up(1, mid_b, tiles_b, table_b)
@@ -434,8 +436,6 @@
     @pl.when(has_next)
     def _():
         deliver(1, mid_b, table_b, pick_b, grad_out, 1, 1 + quarter)
-
-    chains(1)
 
     @pl.when(has_next)
     def _():

time: 93.8 us -> 92.6 us (0.987)
  no operation moved by 1% of the time
where the time goes in v5:
time: 92.6 us; the launch traced here: 92.4 us
  Pallas kernels  91.7 us (99%)
    pallas_call x1, Pallas kernels, on_device(): pl.pallas_call(functools.partial(kernel, sections, peers, cap), out_shape...  89.3 us
    pallas_call x1, Pallas kernels, on_device(): pl.pallas_call(place, out_shape=shapes, in_specs=[in_hbm] * 5, out_specs=...  2.41 us

profile of v5, /device:TPU:7, one launch (start us, length us, event | category | flops | bytes accessed | tf_op | source)
XLA Modules:
  0.0 92.4 jit_solution(16639507950225738294)
XLA Ops:
  0.6 89.3 %adapter_relay.1 = (bf16[3,64,2560]{2,1,0:T(8,128)(2,1)}, bf16[3,64,2560]{2,1,0:T(8,128)(2,1)}, f32[80,128]{1,0:T(8,128)}, f32[80,128]{1,0:T(8,128)}, f32[1,80]{1,0:T(1,128)}) custom-call(s32[2]{0:T(128)} %bitcast.17, s32[2]{0:T(128)} %bitcast.18, s32[2]{0:T(128)} %bitcast.19, bf16[128,2560]{1,0:T(8,128)(2,1)} %bitcast.13, bf16[128,2560]{1,0:T(8,128)(2,1)} %bitcast.14, ...), custom_call_target="tpu_custom_call" | custom-call | flops 503316480 | bytes 2621440 | tf_op jit(solution)/shard_map/adapter_relay/pallas_call | solution.py:563
  90.0 2.4 %place_results.1 = (bf16[3,64,2560]{2,1,0:T(8,128)(2,1)}, bf16[3,64,2560]{2,1,0:T(8,128)(2,1)}, f32[80,128]{1,0:T(8,128)}, f32[80,128]{1,0:T(8,128)}, f32[1,80]{1,0:T(1,128)}) custom-call(bf16[3,64,2560]{2,1,0:T(8,128)(2,1)} %get-tuple-element.15.refs_0_, bf16[3,64,2560]{2,1,0:T(8,128)(2,1)} %get-tuple-element.16.refs_1_, ...), custom_call_target="tpu_custom_call" | custom-call | tf_op jit(solution)/shard_map/place_results/pallas_call | solution.py:603
